TPU v7x, 256 devices: a whole 4x4x8 slice. The times are simulated.
256 devices in a mesh: col: 16 (over z, y_lo), chi: 16 (over y_hi, x, core).
Axes of the slice: x: 4, y: 4 (y_hi: 2, y_lo: 2; y = y_hi * 2 + y_lo), z: 8, core: 2. Of those that a mesh axis runs over, the one named last changes fastest.
Arguments:
- left_iso: bfloat16 [16, 256, 20, 256], P('col', 'chi'), may hold values from -0.078125 to 0.078125
- right_iso: bfloat16 [16, 256, 20, 256], P('col', 'chi'), may hold values from -0.078125 to 0.078125
- center: bfloat16 [16, 256, 20, 256], P('col', 'chi'), may hold values from -0.0048828125 to 0.0048828125
- site_tensor: bfloat16 [16, 400, 400], P('col'), may hold values from -0.3125 to 0.3125
- left_env: float32 [16, 256, 20, 256], P('col', 'chi'), may hold values from -6 to 6
- right_env: float32 [16, 256, 20, 256], P('col', 'chi'), may hold values from -6 to 6
Outputs:
- new_left: float32 [16, 256, 20, 256], P('col', 'chi')
- new_right: float32 [16, 256, 20, 256], P('col', 'chi')
- new_center: float32 [16, 256, 20, 256], P('col', 'chi')
All inputs are finite; a program needn't handle non-finite values.
Results may differ from a plain program's by a relative error of at most 0.011.
Values may be sent and summed in bfloat16 or wider, within the bound.
A program may use at most 64 MiB of HBM per device.

v0:
```python
import jax
import jax.numpy as jnp
from jax import lax
from jax.sharding import PartitionSpec as P


def passed_along(x, axis, by):
    peers = lax.axis_size(axis)
    return lax.ppermute(x, axis, [(i, (i + by) % peers) for i in range(peers)])


def on_device(left_iso, right_iso, center, site_tensor, left_env, right_env):
    left_own = left_iso[0]
    right_own = right_iso[0]
    center_own = center[0]
    site_flat = site_tensor[0]
    row_count = left_own.shape[0]
    bond_width = left_own.shape[1]
    site_four = site_flat.reshape(bond_width, bond_width, bond_width, bond_width)
    left_full, right_full, center_full = (
        lax.all_gather(left_own, "chi", axis=0, tiled=True),
        lax.all_gather(right_own, "chi", axis=0, tiled=True),
        lax.all_gather(center_own, "chi", axis=0, tiled=True),
    )
    chi_span = left_full.shape[0]
    offset = lax.axis_index("chi") * row_count
    left_b = left_env[0].astype(jnp.bfloat16)
    right_b = right_env[0].astype(jnp.bfloat16)
    left_one = jnp.einsum(
        "bla,auc->bluc", left_b, left_full, preferred_element_type=jnp.float32
    ).astype(jnp.bfloat16)
    left_one = left_one.reshape(row_count, bond_width * bond_width, chi_span)
    left_two = jnp.einsum(
        "bpc,pq->bqc", left_one, site_flat, preferred_element_type=jnp.float32
    ).astype(jnp.bfloat16)
    left_two = left_two.reshape(row_count, bond_width, bond_width, chi_span)
    piece = left_own
    left_raw = lax.psum_scatter(
        jnp.einsum("bdc,brda->cra", piece, left_two, preferred_element_type=jnp.float32),
        "chi",
        scatter_dimension=0,
        tiled=True,
    )
    right_one = jnp.einsum(
        "kre,aue->krua", right_b, right_full, preferred_element_type=jnp.float32
    ).astype(jnp.bfloat16)
    right_two = jnp.einsum(
        "krua,lurd->klda", right_one, site_four, preferred_element_type=jnp.float32
    ).astype(jnp.bfloat16)
    right_cols = lax.dynamic_slice_in_dim(right_full, offset, row_count, 2)
    piece = right_cols
    right_raw = lax.psum_scatter(
        jnp.einsum("bdk,klda->bla", piece, right_two, preferred_element_type=jnp.float32),
        "chi",
        scatter_dimension=0,
        tiled=True,
    )
    left_total, right_total = lax.psum(
        (jnp.sum(left_raw * left_raw), jnp.sum(right_raw * right_raw)), "chi"
    )
    entries = float(chi_span * bond_width * chi_span)
    left_new = passed_along(
        (left_raw * jnp.sqrt(entries / left_total)).astype(jnp.bfloat16), "col", 1
    ).astype(jnp.float32)
    right_new = passed_along(
        (right_raw * jnp.sqrt(entries / right_total)).astype(jnp.bfloat16), "col", -1
    ).astype(jnp.float32)
    left_nb = left_new.astype(jnp.bfloat16)
    right_nb = right_new.astype(jnp.bfloat16)
    center_one = jnp.einsum(
        "bla,auc->bluc", left_nb, center_full, preferred_element_type=jnp.float32
    ).astype(jnp.bfloat16)
    center_one = center_one.reshape(row_count, bond_width * bond_width, chi_span)
    center_two = jnp.einsum(
        "bpc,pq->bqc", center_one, site_flat, preferred_element_type=jnp.float32
    ).astype(jnp.bfloat16)
    center_two = center_two.reshape(row_count, bond_width, bond_width, chi_span)
    center_new = jnp.einsum(
        "brda,era->bde",
        center_two,
        lax.all_gather(right_nb, "chi", axis=0, tiled=True),
        preferred_element_type=jnp.float32,
    )
    return (left_new[None], right_new[None], center_new[None])


def solution(mesh):
    return jax.shard_map(
        on_device,
        mesh=mesh,
        in_specs=(
            P("col", "chi", None, None),
            P("col", "chi", None, None),
            P("col", "chi", None, None),
            P("col", None, None),
            P("col", "chi", None, None),
            P("col", "chi", None, None),
        ),
        out_specs=(
            P("col", "chi", None, None),
            P("col", "chi", None, None),
            P("col", "chi", None, None),
        ),
        check_vma=False,
    )
```

profile of v0, /device:TPU:1, one launch (start us, length us, event | category | flops | bytes accessed | tf_op | source)
XLA Modules:
  0.0 457.9 jit_solution(17632268849836748972)
XLA Ops:
  9.7 62.0 %all-gather.10.cloned.1.call-done = bf16[1,256,20,256]{3,1,2,0:T(8,128)(2,1)} async-done(((bf16[1,16,20,256]{3,1,2,0:T(8,128)(2,1)}), bf16[1,256,20,256]{3,1,2,0:T(8,128)(2,1)}) %all-gather.10.cloned.1.call-update) | async-done | bytes 2621456 | tf_op jit(solution)/shard_map/all_gather | solution.py:21
  71.7 2.9 fusion.18
  74.7 1.9 copy.67
  76.6 2.3 convert_bitcast_fusion.2
  80.2 3.9 convolution_bitcast_fusion
  84.1 6.4 %copy.71 = f32[256,20,256]{2,1,0:T(8,128)} copy(f32[256,20,256]{0,2,1:T(8,128)} %convolution_bitcast_fusion) | data formatting | bytes 10485760 | tf_op jit(solution)/shard_map/bdc,brda->cra/dot_general | solution.py:39
  90.8 1.9 reshape_squeeze.3
  92.7 37.3 %all-gather.12.cloned.1.call-done = bf16[1,256,20,256]{3,1,2,0:T(8,128)(2,1)} async-done(((bf16[1,16,20,256]{3,1,2,0:T(8,128)(2,1)}), bf16[1,256,20,256]{3,1,2,0:T(8,128)(2,1)}) %all-gather.12.cloned.1.call-update) | async-done | bytes 2621456 | tf_op jit(solution)/shard_map/all_gather | solution.py:22
  130.0 3.0 convert_bitcast_fusion
  133.0 2.6 fusion
  135.6 4.9 %fusion.29 = f32[256,20,256]{2,0,1:T(8,128)} fusion(bf16[16,20,20,256]{3,2,0,1:T(8,128)(2,1)S(1)} %fusion, bf16[1,256,20,256]{3,1,2,0:T(8,128)(2,1)S(1)} %copy-done, s32[]{:T(128)S(6)} %select_n.3), kind=kOutput, calls=%fused_computation.25 | convolution fusion | flops 838860800 | bytes 10485764 | tf_op jit(solution)/shard_map/bdk,klda->bla/dot_general | solution.py:53
  141.1 87.8 %reduce-scatter.3.cloned.1.call-done = f32[16,20,256]{2,1,0:T(8,128)} async-done(((f32[256,20,256]{2,1,0:T(8,128)}), f32[16,20,256]{2,1,0:T(8,128)}) %reduce-scatter.3.cloned.1.call-update) | async-done | bytes 327696 | tf_op jit(solution)/shard_map/reduce_scatter | solution.py:38
  228.9 1.7 multiply_reduce_fusion
  230.6 94.0 %reduce-scatter.5.cloned.1.call-done = f32[16,20,256]{2,0,1:T(8,128)} async-done(((f32[256,20,256]{2,0,1:T(8,128)}), f32[16,20,256]{2,0,1:T(8,128)}) %reduce-scatter.5.cloned.1.call-update) | async-done | bytes 327696 | tf_op jit(solution)/shard_map/reduce_scatter | solution.py:52
  324.6 1.7 multiply_reduce_fusion.1
  326.2 35.1 %all-reduce = (f32[]{:T(128)}, f32[]{:T(128)}) all-reduce(f32[]{:T(128)} %multiply_reduce_fusion, f32[]{:T(128)} %multiply_reduce_fusion.1), channel_id=1, replica_groups=mesh['col'=16,'chi'=16] {'chi'}, use_global_device_ids=true, to_apply=%region_2.0 | all-reduce | flops 2 | bytes 16 | tf_op jit(solution)/shard_map/psum | solution.py:58
  363.1 3.1 collective-permute-start.1
  366.2 5.8 %collective-permute-done.1 = bf16[16,20,256]{2,0,1:T(8,128)(2,1)S(1)} collective-permute-done((bf16[16,20,256]{2,0,1:T(8,128)(2,1)S(1)}, bf16[16,20,256]{2,0,1:T(8,128)(2,1)S(1)}, u32[]{:S(2)}, u32[]{:S(2)}) %collective-permute-start.1) | collective-permute-done | bytes 163872 | tf_op jit(solution)/shard_map/ppermute | solution.py:9
  374.9 13.2 %all-gather.14.cloned.1.call-done = bf16[1,256,20,256]{3,1,2,0:T(8,128)(2,1)} async-done(((bf16[1,16,20,256]{3,1,2,0:T(8,128)(2,1)}), bf16[1,256,20,256]{3,1,2,0:T(8,128)(2,1)}) %all-gather.14.cloned.1.call-update) | async-done | bytes 2621456 | tf_op jit(solution)/shard_map/all_gather | solution.py:23
  388.1 2.9 fusion.21
  391.0 1.9 copy.79
  392.9 2.3 convert_bitcast_fusion.1
  398.0 49.5 %all-gather.8.cloned.1.call-done = bf16[256,20,256]{2,0,1:T(8,128)(2,1)} async-done(((bf16[16,20,256]{2,0,1:T(8,128)(2,1)}), bf16[256,20,256]{2,0,1:T(8,128)(2,1)}) %all-gather.8.cloned.1.call-update) | async-done | bytes 2621456 | tf_op jit(solution)/shard_map/all_gather | solution.py:81
  447.5 3.5 fusion.38
  (34 shorter events, 10.4 us)
Async XLA Ops:
  7.2 64.5 %all-gather.10.cloned.1.call-start = ((), (), s32[]{:S(2)}) async-start(), calls=%async_computation.5 | async-start | bytes 2785280 | tf_op jit(solution)/shard_map/all_gather | solution.py:21
  7.9 122.1 %all-gather.12.cloned.1.call-start = ((), (), s32[]{:S(2)}) async-start(), calls=%async_computation.6 | async-start | bytes 2785280 | tf_op jit(solution)/shard_map/all_gather | solution.py:22
  8.6 220.3 %reduce-scatter.3.cloned.1.call-start = ((), (), s32[]{:S(2)}) async-start(), calls=%async_computation.2 | async-start | bytes 6684672 | tf_op jit(solution)/shard_map/reduce_scatter | solution.py:38
  74.6 1.9 copy-start.3
  78.9 1.2 copy-start.5
  90.5 2.1 copy-start.4
  90.6 234.0 %reduce-scatter.5.cloned.1.call-start = ((), (), s32[]{:S(2)}) async-start(), calls=%async_computation.3 | async-start | bytes 5570560 | tf_op jit(solution)/shard_map/reduce_scatter | solution.py:52
  133.0 2.6 copy-start
  140.5 247.6 %all-gather.14.cloned.1.call-start = ((), (), s32[]{:S(2)}) async-start(), calls=%async_computation.7 | async-start | bytes 2785280 | tf_op jit(solution)/shard_map/all_gather | solution.py:23
  141.0 306.5 %all-gather.8.cloned.1.call-start = ((), (), s32[]{:S(2)}) async-start(), calls=%async_computation.4 | async-start | bytes 2785280 | tf_op jit(solution)/shard_map/all_gather | solution.py:81
  363.1 8.9 %collective-permute-start.1 = (bf16[16,20,256]{2,0,1:T(8,128)(2,1)S(1)}, bf16[16,20,256]{2,0,1:T(8,128)(2,1)S(1)}, u32[]{:S(2)}, u32[]{:S(2)}) collective-permute-start(bf16[16,20,256]{2,0,1:T(8,128)(2,1)S(1)} %multiply_convert_fusion), channel_id=1, source_target_pairs={{0,240},{16,0},{32,16},{48,32},{64,48},{80,64},{96,80},{112,96},{1... | collective-permute-start | bytes 491528 | tf_op jit(solution)/shard_map/ppermute | solution.py:9
  372.0 0.7 copy-start.1
  374.5 13.5 %collective-permute-start = (bf16[16,20,256]{2,0,1:T(8,128)(2,1)S(1)}, bf16[16,20,256]{2,0,1:T(8,128)(2,1)S(1)}, u32[]{:S(2)}, u32[]{:S(2)}) collective-permute-start(bf16[16,20,256]{2,0,1:T(8,128)(2,1)S(1)} %fusion.43), channel_id=1, source_target_pairs={{0,16},{16,32},{32,48},{48,64},{64,80},{80,96},{96,112},{112,128},... | collective-permute-start | bytes 491528 | tf_op jit(solution)/shard_map/ppermute | solution.py:9
  395.3 1.2 copy-start.2
Sparse Core Ops, SparseCore 0:
  10.6 61.1 all-gather.9
  74.3 55.6 all-gather.11
  134.4 94.4 reduce-scatter.2
  233.1 91.4 reduce-scatter.4
  327.0 61.0 all-gather.13
  391.1 56.3 all-gather.7
where the time goes:
time: 458 us
  waiting for transfers between devices  352 us (77%)
  blocking collectives  35.1 us (8%)
  matrix products  28.4 us (6%)
  between operations  15.7 us (3%)
  local copies, waits for them, and re-layouts  15.2 us (3%)
  other arithmetic  7.98 us (2%)
    reduce_scatter x1, waiting for transfers between devices, on_device(): lax.psum_scatter(jnp.einsum('bdk,klda->bla', piece, right_two, preferred_...  94 us
    reduce_scatter x1, waiting for transfers between devices, on_device(): lax.psum_scatter(jnp.einsum('bdc,brda->cra', piece, left_two, preferred_e...  87.8 us
    all_gather x1, waiting for transfers between devices, on_device(): lax.all_gather(left_own, 'chi', axis=0, tiled=True)  62 us
    all_gather x1, waiting for transfers between devices, on_device(): lax.all_gather(right_nb, 'chi', axis=0, tiled=True)  49.5 us
    all_gather x1, waiting for transfers between devices, on_device(): lax.all_gather(right_own, 'chi', axis=0, tiled=True)  37.3 us
    psum x1, blocking collectives, on_device(): lax.psum((jnp.sum(left_raw * left_raw), jnp.sum(right_raw * right_raw)),...  35.1 us
    all_gather x1, waiting for transfers between devices, on_device(): lax.all_gather(center_own, 'chi', axis=0, tiled=True)  13.2 us
  transfers between devices with their start and end apart: 8, of which 7 were waited for; matrix products, arithmetic and copies ran while one was open for 10% of the time, Pallas kernels for 0%

commit v1 on v0

v1 whole, which is shorter than its diff:
```python
import jax
import jax.numpy as jnp
from jax import lax
from jax.experimental import pallas as pl
from jax.experimental.pallas import tpu as pltpu
from jax.sharding import PartitionSpec as P

MESH = pl.DeviceIdType.MESH
BF = jnp.bfloat16
F32 = jnp.float32
D = 20
DP = 24
CHI = 256
ROWS = 16
HALF = 128
NT = (((1,), (1,)), ((), ()))
NN = (((1,), (0,)), ((), ()))


def dot(a, b, dims=NN):
    return lax.dot_general(a, b, dims, preferred_element_type=F32)


def kernel(
    al_ref, ar_ref, ac_ref, w_ref, l_ref, r_ref,
    new_left_ref, new_right_ref, new_center_ref,
    pad, half_al, half_ar, half_ac, half_r,
    g_al, g_ar, g_ac, g_r, g_n,
    lb, arj, al24, alt, w2, w4, xs, ys, acc, zf, zk,
    sib_s, sib_r, x_s, x_r, raw, lp, lr, ln,
    ry_s, ry_r, rp, rn_r, cy_s, cy_r, sq_s, sq_r,
    send_sem, recv_sem,
):
    col = lax.axis_index("col")
    me = lax.axis_index("chi")
    y, x, c = me // 8, (me // 2) % 4, me % 2
    cols = lax.axis_size("col")

    def at(dcol=0, dy=0, dx=0, dc=0):
        chi = ((y + dy) % 2) * 8 + ((x + dx) % 4) * 2 + (c + dc) % 2
        return ((col + dcol + cols) % cols, chi)

    SIB, YP = at(dc=1), at(dy=1)
    XP = [at(dx=d) for d in (1, 2, 3)]

    barrier = pltpu.get_barrier_semaphore()
    peers = [SIB, YP] + XP + [at(1), at(1, 1), at(-1), at(-1, 1)]
    for p in peers:
        pl.semaphore_signal(barrier, inc=1, device_id=p, device_id_type=MESH)

    count = [0]
    started = []

    def send(src, dst, target):
        i = count[0]
        count[0] += 1
        cp = pltpu.make_async_remote_copy(
            src_ref=src, dst_ref=dst, send_sem=send_sem.at[i], recv_sem=recv_sem.at[i],
            device_id=target, device_id_type=MESH,
        )
        cp.start()
        started.append(cp)
        return cp

    def recv(cps):
        for cp in cps if isinstance(cps, list) else [cps]:
            cp.wait_recv()

    def sent(cp):
        cp.wait_send()
        started[:] = [s for s in started if s is not cp]

    def to_pad(ref):
        for a in range(ROWS):
            v = ref[a].astype(F32)
            pad[0, a * DP:a * DP + D, :] = v[:, :HALF]
            pad[1, a * DP:a * DP + D, :] = v[:, HALF:]

    def padded():
        return jnp.concatenate([pad[0], pad[1]], axis=1)

    def row(h, u):
        return pad[h, pl.ds(u, ROWS, stride=DP), :]

    def halves(g, half):
        for u in range(D):
            for h in range(2):
                half[h, u] = row(h, u).astype(BF)
        g[c, y, x] = half[y]

    def to_x(ref):
        return [send(ref, ref, p) for p in XP]

    def to_y(g, half):
        return send(half.at[1 - y], g.at[c, y, x], YP)

    def own_x(g):
        return to_x(g.at[c, y, x])

    def rest_x(g, first):
        recv(first)
        return to_x(g.at[c, 1 - y, x])

    def to_sib(g, xs_):
        recv(xs_)
        return send(g.at[c], g.at[c], SIB)

    pad[...] = jnp.zeros_like(pad)
    to_pad(al_ref)
    halves(g_al, half_al)
    al24[0] = padded().astype(BF)
    pl.semaphore_wait(barrier, len(peers))
    al_y = to_y(g_al, half_al)
    al_x = own_x(g_al)
    to_pad(r_ref)
    halves(g_r, half_r)
    r_y = to_y(g_r, half_r)
    al_x += rest_x(g_al, al_y)
    r_x = own_x(g_r)
    to_pad(l_ref)
    lb[0] = padded().astype(BF)
    lb_y = send(lb.at[0], lb.at[1], YP)
    al24_y = send(al24.at[0], al24.at[1], YP)
    alt[:, :384] = al24[0].astype(F32).T.astype(BF)
    r_x += rest_x(g_r, r_y)
    to_pad(ar_ref)
    halves(g_ar, half_ar)
    arj[0] = padded().astype(BF)
    ar_y = to_y(g_ar, half_ar)
    arj_y = send(arj.at[0], arj.at[1], YP)
    to_pad(ac_ref)
    halves(g_ac, half_ac)
    ac_y = to_y(g_ac, half_ac)

    def spread(other):
        i = lax.broadcasted_iota(jnp.int32, (D * DP, D * D), 0)
        j = lax.broadcasted_iota(jnp.int32, (D * DP, D * D), 1)
        big = (i * 2731) >> 16
        small = i - big * DP
        want = small * D + big if other else big * D + small
        return jnp.where((small < D) & (j == want), 1.0, 0.0).astype(BF)

    t = dot(spread(True), w_ref[...]).astype(BF)
    w4[...] = dot(t, spread(False), NT).astype(BF)
    w2[...] = w4[...].astype(F32).T.astype(BF)

    def full_rows(g, u):
        return jnp.concatenate(
            [g[cc, yy, xx, u] for yy in range(2) for xx in range(4) for cc in range(2)], axis=0
        )

    def pair_half(g, u2):
        return jnp.concatenate([full_rows(g, 2 * u2), full_rows(g, 2 * u2 + 1)], axis=1)

    def step_one(lhs_ref, g):
        def body(u2, _):
            rhs = pair_half(g, u2)
            for k in range(2):
                out = dot(lhs_ref[k], rhs)
                xs[u2, 16 * k:16 * k + 16] = out.reshape(16, DP, CHI)
            return 0
        lax.fori_loop(0, D // 2, body, 0)

    def step_two(m_ref):
        def body(p, _):
            rows = []
            for u2 in range(D // 2):
                v0, v1 = xs[u2, 2 * p], xs[u2, 2 * p + 1]
                rows.append(jnp.concatenate([v0[:, :HALF], v1[:, :HALF]], axis=1))
                rows.append(jnp.concatenate([v0[:, HALF:], v1[:, HALF:]], axis=1))
            rhs = jnp.concatenate(rows, axis=0).astype(BF)
            out = dot(m_ref[...], rhs)
            for r2 in range(D // 2):
                o0 = out[2 * r2 * DP:(2 * r2 + 1) * DP]
                o1 = out[(2 * r2 + 1) * DP:(2 * r2 + 2) * DP]
                top = jnp.concatenate([o0[:, :HALF], o1[:, :HALF]], axis=1)
                low = jnp.concatenate([o0[:, HALF:], o1[:, HALF:]], axis=1)
                ys[r2, p] = jnp.concatenate([top, low], axis=0).astype(BF)
            return 0
        lax.fori_loop(0, 16, body, 0)

    def step_three(g):
        acc[...] = jnp.zeros_like(acc)

        def body(n2, _):
            rhs = pair_half(g, n2)
            for k in range(2):
                lhs = ys[n2, 8 * k:8 * k + 8].reshape(384, CHI)
                acc[k] += dot(lhs, rhs, NT)
            return 0
        lax.fori_loop(0, D // 2, body, 0)

    def sum_all(part, slot):
        sq_s[slot, 0] = part
        cp = send(sq_s.at[slot, 0], sq_r.at[slot, 0], SIB)
        recv(cp)
        part = part + sq_r[slot, 0]
        sq_s[slot, 1] = part
        cp = send(sq_s.at[slot, 1], sq_r.at[slot, 1], YP)
        recv(cp)
        part = part + sq_r[slot, 1]
        sq_s[slot, 2] = part
        cps = [send(sq_s.at[slot, 2], sq_r.at[slot, 2 + d], XP[d]) for d in range(3)]
        recv(cps)
        part = part + sq_r[slot, 2] + sq_r[slot, 3] + sq_r[slot, 4]
        total = jnp.sum(part)
        return jnp.sqrt(float(CHI * D * CHI) / total)

    al_sib = to_sib(g_al, al_x)
    ar_x = own_x(g_ar) + rest_x(g_ar, ar_y)
    recv([al24_y, lb_y, al_sib])
    alt[:, 384:] = al24[1].astype(F32).T.astype(BF)
    step_one(lb, g_al)
    step_two(w2)
    sib = []
    for ch in range(2):
        def body(k, _):
            r2 = ch * 5 + k
            zf[...] = dot(alt[...], ys[r2].reshape(768, CHI)).reshape(8, 2, ROWS, CHI)
            sib_s[r2] = zf[:, 1 - c].astype(BF)
            zk[r2] = zf[:, c]
            return 0
        lax.fori_loop(0, 5, body, 0)
        part_of = pl.ds(ch * 5, 5)
        sib.append(send(sib_s.at[part_of], sib_r.at[part_of], SIB))
    rs = []
    for ch in range(2):
        recv(sib[ch])
        for k in range(5):
            r2 = ch * 5 + k
            v = zk[r2] + sib_r[r2].astype(F32)
            zk[r2] = v
            for yy in range(2):
                for xx in range(4):
                    x_s[xx, r2, yy] = v[yy * 4 + xx].astype(BF)
        part_of = pl.ds(ch * 5, 5)
        for d in (1, 2, 3):
            to = (x + d) % 4
            rs.append(send(x_s.at[to, part_of], x_r.at[d - 1, part_of], XP[d - 1]))
    r_sib = to_sib(g_r, r_x)
    ac_x = own_x(g_ac) + rest_x(g_ac, ac_y)
    recv([arj_y, r_sib])
    step_one(arj, g_r)
    recv(rs)
    part = jnp.zeros((8, HALF), F32)
    for r2 in range(D // 2):
        for yy in range(2):
            v = zk[r2, yy * 4 + x]
            for d in range(3):
                v = v + x_r[d, r2, yy].astype(F32)
            raw[r2, yy] = v
            s = v * v
            s = s[:, :HALF] + s[:, HALF:]
            part = part + s[:8] + s[8:]
    scale = sum_all(part, 1)
    lp[...] = (raw[...] * scale).astype(BF)
    l_col = [send(lp, lr.at[y], at(1)), send(lp, lr.at[y], at(1, 1))]

    step_two(w4)
    ar_sib = to_sib(g_ar, ar_x)
    recv(ar_sib)
    step_three(g_ar)
    ry_s[...] = acc[1].astype(BF)
    ry = send(ry_s, ry_r, YP)
    ac_sib = to_sib(g_ac, ac_x)
    recv(ry)
    right = acc[0] + ry_r[...].astype(F32)
    pad[0] = right[:, :HALF]
    pad[1] = right[:, HALF:]
    sqr = right * right
    part = jnp.sum((sqr[:, :HALF] + sqr[:, HALF:]).reshape(48, 8, HALF), axis=0)
    scale = sum_all(part, 0)
    for h in range(2):
        for u in range(D):
            rp[h, u] = (row(h, u) * scale).astype(BF)
    n_own = send(rp.at[y], g_n.at[c, y, x], at(-1))
    n_other = send(rp.at[1 - y], g_n.at[c, y, x], at(-1, 1))
    n_rest = send(rp.at[1 - y], rn_r, at(-1))

    recv(l_col)
    sent(lb_y)
    ln[...] = jnp.zeros_like(ln)
    for yy in range(2):
        for src in range(2):
            for l in range(D):
                h = l % 2
                v = lr[src, l // 2, yy, :, h * HALF:(h + 1) * HALF].astype(F32)
                ln[yy, src, pl.ds(l, ROWS, stride=DP), :] = v
    for yy in range(2):
        lb[yy] = jnp.concatenate([ln[yy, 0], ln[yy, 1]], axis=1).astype(BF)
    recv(ac_sib)
    step_one(lb, g_ac)
    recv([n_own, n_other])
    n_x = own_x(g_n) + to_x(g_n.at[c, 1 - y, x])
    step_two(w2)
    n_sib = to_sib(g_n, n_x)
    lnew = jnp.concatenate([ln[y, 0], ln[y, 1]], axis=1)
    new_left_ref[...] = lnew.reshape(ROWS, DP, CHI)[:, :D]
    recv(n_rest)
    for l in range(D):
        pad[y, pl.ds(l, ROWS, stride=DP), :] = g_n[c, y, x, l].astype(F32)
        pad[1 - y, pl.ds(l, ROWS, stride=DP), :] = rn_r[l].astype(F32)
    new_right_ref[...] = padded().reshape(ROWS, DP, CHI)[:, :D]
    recv(n_sib)
    step_three(g_n)
    cy_s[...] = acc[1 - y].astype(BF)
    cy = send(cy_s, cy_r, YP)
    recv(cy)
    center = acc[y] + cy_r[...].astype(F32)
    new_center_ref[...] = center.reshape(ROWS, DP, CHI)[:, :D]
    for cp in started:
        cp.wait_send()


def on_device(left_iso, right_iso, center, site_tensor, left_env, right_env):
    out = jax.ShapeDtypeStruct((ROWS, D, CHI), F32)
    vm = pl.BlockSpec(memory_space=pltpu.VMEM)
    V = pltpu.VMEM
    res = pl.pallas_call(
        kernel,
        out_shape=[out] * 3,
        in_specs=[vm] * 6,
        out_specs=[vm] * 3,
        scratch_shapes=[
            V((2, ROWS * DP, HALF), F32),
            *[V((2, D, ROWS, HALF), BF)] * 4,
            *[V((2, 2, 4, D, ROWS, HALF), BF)] * 5,
            *[V((2, ROWS * DP, CHI), BF)] * 3,
            V((CHI, 2 * ROWS * DP), BF),
            V((D * DP, D * DP), BF), V((D * DP, D * DP), BF),
            V((D // 2, 32, DP, CHI), F32),
            V((D // 2, 16, 2 * DP, CHI), BF),
            V((2, ROWS * DP, CHI), F32),
            V((8, 2, ROWS, CHI), F32),
            V((D // 2, 8, ROWS, CHI), F32),
            V((D // 2, 8, ROWS, CHI), BF), V((D // 2, 8, ROWS, CHI), BF),
            V((4, D // 2, 2, ROWS, CHI), BF), V((3, D // 2, 2, ROWS, CHI), BF),
            V((D // 2, 2, ROWS, CHI), F32),
            V((D // 2, 2, ROWS, CHI), BF), V((2, D // 2, 2, ROWS, CHI), BF),
            V((2, 2, ROWS * DP, HALF), F32),
            V((ROWS * DP, CHI), BF), V((ROWS * DP, CHI), BF),
            V((2, D, ROWS, HALF), BF), V((D, ROWS, HALF), BF),
            V((ROWS * DP, CHI), BF), V((ROWS * DP, CHI), BF),
            V((2, 3, 8, HALF), F32), V((2, 5, 8, HALF), F32),
            pltpu.SemaphoreType.DMA((72,)), pltpu.SemaphoreType.DMA((72,)),
        ],
        compiler_params=pltpu.CompilerParams(
            collective_id=0, has_side_effects=True, vmem_limit_bytes=56 * 2**20
        ),
        cost_estimate=pl.CostEstimate(flops=9 * 10**9, bytes_accessed=3 * 10**6, transcendentals=0),
        name="vumps",
    )(left_iso[0], right_iso[0], center[0], site_tensor[0], left_env[0], right_env[0])
    return tuple(o[None] for o in res)


def solution(mesh):
    spec = P("col", "chi", None, None)
    return jax.shard_map(
        on_device,
        mesh=mesh,
        in_specs=(spec, spec, spec, P("col", None, None), spec, spec),
        out_specs=(spec, spec, spec),
        check_vma=False,
    )
```

time: 458 us -> 116 us (0.25)
  waiting for transfers between devices: 352 us -> 0 us
  Pallas kernels: 0 us -> 107 us
  blocking collectives: 35.1 us -> 0 us
  matrix products: 28.4 us -> 0 us
  between operations: 15.7 us -> 0.67 us
  other arithmetic: 7.98 us -> 0 us
  local copies, waits for them, and re-layouts: 15.2 us -> 7.87 us
    reduce_scatter x2 -> x0, waiting for transfers between devices: 182 us -> none  [the longest x1 94 us: on_device(): lax.psum_scatter(jnp.einsum('bdk,klda->bla', piece, right_two, preferred_...]
    all_gather x4 -> x0, waiting for transfers between devices: 162 us -> none  [the longest x1 62 us: on_device(): lax.all_gather(left_own, 'chi', axis=0, tiled=True)]
    pallas_call x0 -> x1, Pallas kernels: none -> 107 us  [on_device(): pl.pallas_call(kernel, out_shape=[out] * 3, in_specs=[vm] * 6, out_specs=...]
    psum x1 -> x0, blocking collectives: 35.1 us -> none  [on_device(): lax.psum((jnp.sum(left_raw * left_raw), jnp.sum(right_raw * right_raw)),...]
    dot_general x9 -> x0, matrix products: 28.4 us -> none  [the longest x1 4.88 us: on_device(): jnp.einsum('bdk,klda->bla', piece, right_two, preferred_element_type=jnp....]
    dot_general x1 -> x0, local copies, waits for them, and re-layouts: 6.43 us -> none  [on_device(): jnp.einsum('bdc,brda->cra', piece, left_two, preferred_element_type=jnp.f...]
    convert_element_type x4 -> x0, local copies, waits for them, and re-layouts: 6.22 us -> none  [the longest x1 1.89 us: on_device(): left_one = jnp.einsum('bla,auc->bluc', left_b, left_full, preferred_eleme...]
    ppermute x2 -> x0, waiting for transfers between devices: 5.8 us -> none  [passed_along(): return lax.ppermute(x, axis, [(i, (i + by) % peers) for i in range(peers)])]
  transfers between devices with their start and end apart: 8 -> 0, of which waited for: 7 -> 0; matrix products, arithmetic and copies ran while one was open for 10% -> 0% of each run, Pallas kernels for 0% -> 0%
where the time goes in v1:
time: 116 us; the launch traced here: 115 us
  Pallas kernels  107 us (92%)
  local copies, waits for them, and re-layouts  7.87 us (7%)
    pallas_call x1, Pallas kernels, on_device(): pl.pallas_call(kernel, out_shape=[out] * 3, in_specs=[vm] * 6, out_specs=...  107 us
    unnamed x16, local copies, waits for them, and re-layouts  5.76 us

profile of v1, /device:TPU:1, one launch (start us, length us, event | category | flops | bytes accessed | tf_op | source)
XLA Modules:
  0.0 115.3 jit_solution(10460273696497361133)
XLA Ops:
  0.6 0.0 copy-start.4
  0.6 0.0 copy-start.5
  0.7 1.7 %copy.22 = bf16[1,16,20,256]{3,2,1,0:T(8,128)(2,1)} copy(bf16[1,16,20,256]{3,1,2,0:T(8,128)(2,1)} %param.6) | data formatting | bytes 327680 | tf_op args[0]
  2.3 0.0 copy-done.4
  2.3 0.0 copy-done.5
  2.3 0.0 copy-start.2
  2.3 0.0 copy-start.3
  2.4 0.8 copy_bitcast_fusion.2
  3.2 0.1 copy-done.2
  3.3 0.2 copy-done.3
  3.6 1.3 %copy_bitcast_fusion = (f32[16,20,256]{2,1,0:T(8,128)}, f32[16,20,256]{2,1,0:T(8,128)}) fusion(f32[1,16,20,256]{3,1,2,0:T(8,128)S(1)} %copy-done.2, f32[1,16,20,256]{3,1,2,0:T(8,128)S(1)} %copy-done.3), kind=kLoop, calls=%fused_computation | loop fusion | bytes 1310720 | tf_op jit(solution)/shard_map/squeeze | solution.py:352
  4.8 106.8 %vumps.1 = (f32[16,20,256]{2,1,0:T(8,128)}, f32[16,20,256]{2,1,0:T(8,128)}, f32[16,20,256]{2,1,0:T(8,128)}) custom-call(bf16[16,20,256]{2,1,0:T(8,128)(2,1)} %bitcast.18, bf16[16,20,256]{2,1,0:T(8,128)(2,1)} %get-tuple-element.15.ar_ref, bf16[16,20,256]{2,1,0:T(8,128)(2,1)} %get-tuple-element.14.ac_ref, bf16[400,400]{1,0:T(8,128)(2,1)} %bitcast.19, ...), custom_call_target="tpu_custom_call" | custom-call | flops 8999999488 | bytes 3000000 | tf_op jit(solution)/shard_map/vumps/pallas_call | solution.py:319
  111.6 0.0 copy-start.1
  111.6 1.9 %copy.14 = f32[1,16,20,256]{3,1,2,0:T(8,128)} copy(f32[1,16,20,256]{3,2,1,0:T(8,128)} %bitcast.17) | data formatting | bytes 655360
  113.5 0.0 copy-start
  113.5 0.0 copy-done.1
  113.5 0.8 copy.15
  114.4 0.2 copy-done
  114.5 0.8 copy.16
Async XLA Ops:
  0.6 1.7 %copy-start.4 = (bf16[1,16,20,256]{3,1,2,0:T(8,128)(2,1)S(1)}, bf16[1,16,20,256]{3,1,2,0:T(8,128)(2,1)}, u32[]{:S(2)}) copy-start(bf16[1,16,20,256]{3,1,2,0:T(8,128)(2,1)} %param.8) | copy-start | bytes 491524
  0.6 1.7 %copy-start.5 = (bf16[1,16,20,256]{3,1,2,0:T(8,128)(2,1)S(1)}, bf16[1,16,20,256]{3,1,2,0:T(8,128)(2,1)}, u32[]{:S(2)}) copy-start(bf16[1,16,20,256]{3,1,2,0:T(8,128)(2,1)} %param.7) | copy-start | bytes 491524
  2.3 1.0 copy-start.2
  2.3 1.2 %copy-start.3 = (f32[1,16,20,256]{3,1,2,0:T(8,128)S(1)}, f32[1,16,20,256]{3,1,2,0:T(8,128)}, u32[]{:S(2)}) copy-start(f32[1,16,20,256]{3,1,2,0:T(8,128)} %param.10) | copy-start | bytes 983044
  111.6 1.9 %copy-start.1 = (f32[16,20,256]{2,1,0:T(8,128)S(1)}, f32[16,20,256]{2,1,0:T(8,128)}, u32[]{:S(2)}) copy-start(f32[16,20,256]{2,1,0:T(8,128)} %get-tuple-element.7) | copy-start | bytes 983044
  113.5 1.0 copy-start

commit v2 on v1

v2 whole, which is shorter than its diff:
```python
import jax
import jax.numpy as jnp
from jax import lax
from jax.experimental import pallas as pl
from jax.experimental.pallas import tpu as pltpu
from jax.sharding import PartitionSpec as P

MESH = pl.DeviceIdType.MESH
BF = jnp.bfloat16
F32 = jnp.float32
D = 20
DP = 24
CHI = 256
ROWS = 16
HALF = 128
NT = (((1,), (1,)), ((), ()))
NN = (((1,), (0,)), ((), ()))


def dot(a, b, dims=NN):
    return lax.dot_general(a, b, dims, preferred_element_type=F32)


def kernel(
    al_ref, ar_ref, ac_ref, w_ref, l_ref, r_ref,
    new_left_ref, new_right_ref, new_center_ref,
    pad, half_r, p_al, p_ar, lbf, lbp,
    g_al, g_ar, g_ac, g_r, g_n,
    lb, arj, alt, w2, w4, xs, ys, acc, zf, zk,
    sib_s, sib_r, x_s, x_r, raw, lp, lr, ln,
    rs_s, n_in, n_sum, n_snd, n_oth, cy_s, cy_r, sq_s, sq_r, sc_s, sc_r,
    send_sem, recv_sem,
):
    col = lax.axis_index("col")
    me = lax.axis_index("chi")
    y, x, c = me // 8, (me // 2) % 4, me % 2
    cols = lax.axis_size("col")

    def at(dcol=0, dy=0, dx=0, dc=0):
        chi = ((y + dy) % 2) * 8 + ((x + dx) % 4) * 2 + (c + dc) % 2
        return ((col + dcol + cols) % cols, chi)

    SIB, YP = at(dc=1), at(dy=1)
    XP = [at(dx=d) for d in (1, 2, 3)]

    barrier = pltpu.get_barrier_semaphore()
    peers = [SIB, YP] + XP + [at(1), at(1, 1), at(-1), at(-1, 1)]
    for p in peers:
        pl.semaphore_signal(barrier, inc=1, device_id=p, device_id_type=MESH)

    count = [0]
    started = []

    def send(src, dst, target):
        i = count[0]
        count[0] += 1
        cp = pltpu.make_async_remote_copy(
            src_ref=src, dst_ref=dst, send_sem=send_sem.at[i], recv_sem=recv_sem.at[i],
            device_id=target, device_id_type=MESH,
        )
        cp.start()
        started.append(cp)
        return cp

    def recv(cps):
        for cp in cps if isinstance(cps, list) else [cps]:
            cp.wait_recv()

    def own_half(v):
        return jnp.where(y == 0, v[..., :HALF], v[..., HALF:])

    def other_half(v):
        return jnp.where(y == 0, v[..., HALF:], v[..., :HALF])

    def lanes(ref, h):
        return ref.at[:, :, pl.ds(pl.multiple_of(h * HALF, HALF), HALF)]

    def put(h, u, v):
        pad[h, pl.ds(u, ROWS, stride=DP), :] = v.astype(F32)

    def row(h, u):
        return pad[h, pl.ds(u, ROWS, stride=DP), :]

    def padded():
        return jnp.concatenate([pad[0], pad[1]], axis=1)

    def pad_own(ref):
        for u in range(D):
            v = ref[u].astype(F32)
            put(0, u, v[:, :HALF])
            put(1, u, v[:, HALF:])
        return padded()

    def pad_partner(g, p):
        for u in range(D):
            put(y, u, g[c, x, 1 - y, u])
            put(1 - y, u, p[u])
        return padded()

    def to_x(ref):
        return [send(ref, ref, p) for p in XP]

    def to_y(g, src):
        return send(src, g.at[c, x, y], YP)

    def own_x(g):
        return to_x(g.at[c, x, y])

    def rest_x(g, first):
        recv(first)
        return to_x(g.at[c, x, 1 - y])

    def to_sib(g, xs_):
        recv(xs_)
        return send(g.at[c], g.at[c], SIB)

    g_al[c, x, y] = own_half(al_ref[...])
    half_r[...] = other_half(r_ref[...]).astype(BF)
    g_r[c, x, y] = own_half(r_ref[...]).astype(BF)
    pad[...] = jnp.zeros_like(pad)
    pl.semaphore_wait(barrier, len(peers))
    al_y = to_y(g_al, lanes(al_ref, 1 - y))
    al_x = own_x(g_al)
    r_y = to_y(g_r, half_r)
    lbf[...] = l_ref[...].astype(BF)
    lb_y = send(lbf, lbp, YP)
    p_al_y = send(lanes(al_ref, y), p_al, YP)
    ar_y = to_y(g_ar, lanes(ar_ref, 1 - y))
    p_ar_y = send(lanes(ar_ref, y), p_ar, YP)
    ac_y = to_y(g_ac, lanes(ac_ref, 1 - y))
    g_ar[c, x, y] = own_half(ar_ref[...])
    g_ac[c, x, y] = own_half(ac_ref[...])
    al_x += rest_x(g_al, al_y)
    r_x = own_x(g_r) + rest_x(g_r, r_y)
    ar_x = own_x(g_ar)
    lb[0] = pad_own(l_ref).astype(BF)
    alt[:, :384] = pad_own(al_ref).T.astype(BF)
    arj[0] = pad_own(ar_ref).astype(BF)
    ln[...] = jnp.zeros_like(ln)

    def spread(other):
        i = lax.broadcasted_iota(jnp.int32, (D * DP, D * D), 0)
        j = lax.broadcasted_iota(jnp.int32, (D * DP, D * D), 1)
        big = (i * 2731) >> 16
        small = i - big * DP
        want = small * D + big if other else big * D + small
        return jnp.where((small < D) & (j == want), 1.0, 0.0).astype(BF)

    t = dot(spread(True), w_ref[...]).astype(BF)
    w4[...] = dot(t, spread(False), NT).astype(BF)
    w2[...] = w4[...].astype(F32).T.astype(BF)

    def full_rows(g, u):
        return jnp.concatenate(
            [g[cc, xx, yy, u] for yy in range(2) for xx in range(4) for cc in range(2)], axis=0
        )

    def pair_half(g, u2):
        return jnp.concatenate([full_rows(g, 2 * u2), full_rows(g, 2 * u2 + 1)], axis=1)

    def run(n, body, hooks=()):
        begin = 0
        for i, f in list(hooks) + [(n, None)]:
            lax.fori_loop(begin, i, lambda k, _: body(k), None)
            begin = i
            if f is not None:
                f()

    def step_one(lhs_ref, g, hooks=()):
        def body(q):
            rhs = jnp.concatenate([pair_half(g, 5 * q + i) for i in range(5)], axis=1)
            for k in range(2):
                out = dot(lhs_ref[k], rhs)
                for i in range(5):
                    xs[5 * q + i, 16 * k:16 * k + 16] = out[:, i * CHI:(i + 1) * CHI].reshape(16, DP, CHI)
        run(D // 2 // 5, body, hooks)

    def step_two(m_ref, hooks=()):
        def body(q):
            cols_ = []
            for i in range(4):
                p = 4 * q + i
                rows = []
                for u2 in range(D // 2):
                    v0, v1 = xs[u2, 2 * p], xs[u2, 2 * p + 1]
                    rows.append(jnp.concatenate([v0[:, :HALF], v1[:, :HALF]], axis=1))
                    rows.append(jnp.concatenate([v0[:, HALF:], v1[:, HALF:]], axis=1))
                cols_.append(jnp.concatenate(rows, axis=0).astype(BF))
            both = dot(m_ref[...], jnp.concatenate(cols_, axis=1))
            for i in range(4):
                out = both[:, i * CHI:(i + 1) * CHI]
                for r2 in range(D // 2):
                    o0 = out[2 * r2 * DP:(2 * r2 + 1) * DP]
                    o1 = out[(2 * r2 + 1) * DP:(2 * r2 + 2) * DP]
                    top = jnp.concatenate([o0[:, :HALF], o1[:, :HALF]], axis=1)
                    low = jnp.concatenate([o0[:, HALF:], o1[:, HALF:]], axis=1)
                    ys[r2, 4 * q + i] = jnp.concatenate([top, low], axis=0).astype(BF)
        run(16 // 4, body, hooks)

    def step_three(g, k):
        def body(n2):
            lhs = jnp.concatenate([ys[i, pl.ds(8 * k, 8)].reshape(384, CHI) for i in range(10)], axis=1)
            rhs = jnp.concatenate([pair_half(g, i) for i in range(10)], axis=1)
            acc[k] = dot(lhs, rhs, NT)
        body(0)
        pad[0] = acc[k, :, :HALF]
        pad[1] = acc[k, :, HALF:]

    def sum_all(part, slot):
        sq_s[slot, 0] = part
        cp = send(sq_s.at[slot, 0], sq_r.at[slot, 0], SIB)
        recv(cp)
        part = part + sq_r[slot, 0]
        sq_s[slot, 1] = part
        cp = send(sq_s.at[slot, 1], sq_r.at[slot, 1], YP)
        recv(cp)
        part = part + sq_r[slot, 1]
        sq_s[slot, 2] = part
        cps = [send(sq_s.at[slot, 2], sq_r.at[slot, 2 + d], XP[d]) for d in range(3)]
        recv(cps)
        part = part + sq_r[slot, 2] + sq_r[slot, 3] + sq_r[slot, 4]
        total = jnp.sum(part)
        return jnp.sqrt(float(CHI * D * CHI) / total)

    def squares(v):
        s = v * v
        if s.shape[1] > HALF:
            s = s[:, :HALF] + s[:, HALF:]
        return s[:8] + s[8:]

    al_sib = to_sib(g_al, al_x)
    ar_x += rest_x(g_ar, ar_y)
    recv([p_al_y, lb_y])
    alt[:, 384:] = pad_partner(g_al, p_al).T.astype(BF)
    lb[1] = pad_own(lbp).astype(BF)
    recv(al_sib)
    step_one(lb, g_al)
    step_two(w2)
    r_sib = to_sib(g_r, r_x)
    recv(p_ar_y)
    arj[1] = pad_partner(g_ar, p_ar).astype(BF)
    sib = []
    for ch in range(2):
        def z_body(k):
            rhs = jnp.concatenate([ys[ch * 5 + 5 * k + i].reshape(768, CHI) for i in range(5)], axis=1)
            out = dot(alt[...], rhs)
            for i in range(5):
                r2 = ch * 5 + 5 * k + i
                zf[...] = out[:, i * CHI:(i + 1) * CHI].reshape(8, 2, ROWS, CHI)
                sib_s[r2] = zf[:, 1 - c].astype(BF)
                zk[r2] = zf[:, c]
        run(5 // 5, z_body)
        part_of = pl.ds(ch * 5, 5)
        sib.append(send(sib_s.at[part_of], sib_r.at[part_of], SIB))
    rs = []
    for ch in range(2):
        recv(sib[ch])
        for k in range(5):
            r2 = ch * 5 + k
            v = zk[r2] + sib_r[r2].astype(F32)
            zk[r2] = v
            for yy in range(2):
                for xx in range(4):
                    x_s[xx, r2, yy] = v[yy * 4 + xx].astype(BF)
        part_of = pl.ds(ch * 5, 5)
        for d in (1, 2, 3):
            to = (x + d) % 4
            rs.append(send(x_s.at[to, part_of], x_r.at[d - 1, part_of], XP[d - 1]))
    ac_x = own_x(g_ac) + rest_x(g_ac, ac_y)

    recv(r_sib)
    step_one(arj, g_r)
    step_two(w4, [(2, lambda: None)])
    recv(rs)
    part = jnp.zeros((8, HALF), F32)
    for r2 in range(D // 2):
        for yy in range(2):
            v = zk[r2, yy * 4 + x]
            for d in range(3):
                v = v + x_r[d, r2, yy].astype(F32)
            lp[r2, yy] = v.astype(BF)
            part = part + squares(v)
    l_col = [send(lp, lr.at[y], at(1)), send(lp, lr.at[y], at(1, 1))]
    left_part = part
    ar_sib = to_sib(g_ar, ar_x)
    scale = sum_all(left_part, 1)
    sc_s[...] = jnp.full((8, HALF), 1.0, F32) * scale
    l_sc = send(sc_s, sc_r, at(1))
    recv(ar_sib)
    n_col = []
    for k, blk in ((0, y), (1, 1 - y)):
        step_three(g_ar, k)
        for h in range(2):
            for l in range(D):
                rs_s[h, k, l] = row(h, l).astype(BF)
        n_col.append(send(rs_s.at[y, k], n_in.at[y, blk], at(-1)))
        n_col.append(send(rs_s.at[1 - y, k], n_in.at[y, blk], at(-1, 1)))

    ac_sib = to_sib(g_ac, ac_x)
    recv(l_col + [l_sc])
    scale = sc_r[0:1, 0:1]
    for l in range(D):
        h = l % 2
        for src in range(2):
            for yy in range(2):
                v = lr[src, l // 2, yy, :, h * HALF:(h + 1) * HALF].astype(F32) * scale
                ln[yy, src, pl.ds(l, ROWS, stride=DP), :] = v
    for yy in range(2):
        lb[yy] = jnp.concatenate([ln[yy, 0], ln[yy, 1]], axis=1).astype(BF)
    for l in range(D):
        for src in range(2):
            new_left_ref[l, :, src * HALF:(src + 1) * HALF] = ln[y, src, pl.ds(l, ROWS, stride=DP), :]
    recv(ac_sib)
    step_one(lb, g_ac)
    recv(n_col)
    part = jnp.zeros((8, HALF), F32)
    for yy in range(2):
        for l in range(D):
            v = n_in[0, yy, l].astype(F32) + n_in[1, yy, l].astype(F32)
            n_sum[yy, l] = v
            g_n[c, x, yy, l] = v.astype(BF)
            part = part + squares(v)
    n_x = to_x(g_n.at[c, x])
    n_snd[...] = n_sum[1 - y].astype(BF)
    n_y = send(n_snd, n_oth, YP)
    step_two(w2)
    n_sib = to_sib(g_n, n_x)
    scale = sum_all(part, 0)
    recv(n_y)
    for l in range(D):
        a, b = n_sum[y, l] * scale, n_oth[l].astype(F32) * scale
        new_right_ref[l, :, :HALF] = jnp.where(y == 0, a, b)
        new_right_ref[l, :, HALF:] = jnp.where(y == 0, b, a)
    recv(n_sib)
    step_three(g_n, 1 - y)
    cy_s[...] = acc[1 - y].astype(BF)
    cy = send(cy_s, cy_r, YP)
    step_three(g_n, y)
    recv(cy)
    pad[0] = (acc[y, :, :HALF] + cy_r[:, :HALF].astype(F32)) * scale
    pad[1] = (acc[y, :, HALF:] + cy_r[:, HALF:].astype(F32)) * scale
    for n in range(D):
        new_center_ref[n, :, :HALF] = row(0, n)
        new_center_ref[n, :, HALF:] = row(1, n)
    for cp in started:
        cp.wait_send()


def on_device(left_iso, right_iso, center, site_tensor, left_env, right_env):
    out = jax.ShapeDtypeStruct((D, ROWS, CHI), F32)
    vm = pl.BlockSpec(memory_space=pltpu.VMEM)
    V = pltpu.VMEM
    res = pl.pallas_call(
        kernel,
        out_shape=[out] * 3,
        in_specs=[vm] * 6,
        out_specs=[vm] * 3,
        scratch_shapes=[
            V((2, ROWS * DP, HALF), F32),
            *[V((D, ROWS, HALF), BF)] * 3,
            *[V((D, ROWS, CHI), BF)] * 2,
            *[V((2, 4, 2, D, ROWS, HALF), BF)] * 5,
            *[V((2, ROWS * DP, CHI), BF)] * 2,
            V((CHI, 2 * ROWS * DP), BF),
            V((D * DP, D * DP), BF), V((D * DP, D * DP), BF),
            V((D // 2, 32, DP, CHI), F32),
            V((D // 2, 16, 2 * DP, CHI), BF),
            V((2, ROWS * DP, CHI), F32),
            V((8, 2, ROWS, CHI), F32),
            V((D // 2, 8, ROWS, CHI), F32),
            V((D // 2, 8, ROWS, CHI), BF), V((D // 2, 8, ROWS, CHI), BF),
            V((4, D // 2, 2, ROWS, CHI), BF), V((3, D // 2, 2, ROWS, CHI), BF),
            V((8, HALF), F32),
            V((D // 2, 2, ROWS, CHI), BF), V((2, D // 2, 2, ROWS, CHI), BF),
            V((2, 2, ROWS * DP, HALF), F32),
            V((2, 2, D, ROWS, HALF), BF), V((2, 2, D, ROWS, HALF), BF),
            V((2, D, ROWS, HALF), F32),
            V((D, ROWS, HALF), BF), V((D, ROWS, HALF), BF),
            V((ROWS * DP, CHI), BF), V((ROWS * DP, CHI), BF),
            V((2, 3, 8, HALF), F32), V((2, 5, 8, HALF), F32),
            V((8, HALF), F32), V((8, HALF), F32),
            pltpu.SemaphoreType.DMA((72,)), pltpu.SemaphoreType.DMA((72,)),
        ],
        compiler_params=pltpu.CompilerParams(
            collective_id=0, has_side_effects=True, vmem_limit_bytes=56 * 2**20
        ),
        cost_estimate=pl.CostEstimate(flops=9 * 10**9, bytes_accessed=3 * 10**6, transcendentals=0),
        name="vumps",
    )(
        *(v[0].transpose(1, 0, 2) for v in (left_iso, right_iso, center)),
        site_tensor[0],
        *(v[0].transpose(1, 0, 2) for v in (left_env, right_env)),
    )
    return tuple(o.transpose(1, 0, 2)[None] for o in res)


def solution(mesh):
    spec = P("col", "chi", None, None)
    return jax.shard_map(
        on_device,
        mesh=mesh,
        in_specs=(spec, spec, spec, P("col", None, None), spec, spec),
        out_specs=(spec, spec, spec),
        check_vma=False,
    )
```

time: 116 us -> 88.6 us (0.76)
  Pallas kernels: 107 us -> 82.9 us
  local copies, waits for them, and re-layouts: 7.87 us -> 3.58 us
    pallas_call x1, Pallas kernels: 107 us -> 82.9 us  [on_device(): pl.pallas_call(kernel, out_shape=[out] * 3, in_specs=[vm] * 6, out_specs=...]
    unnamed x16 -> x7, local copies, waits for them, and re-layouts: 5.76 us -> 3.58 us
    squeeze x2 -> x0, local copies, waits for them, and re-layouts: 2.11 us -> none  [the longest x1 1.27 us: on_device(): right_env[0]]
where the time goes in v2:
time: 88.6 us; the launch traced here: 87.2 us
  Pallas kernels  82.9 us (94%)
  local copies, waits for them, and re-layouts  3.58 us (4%)
    pallas_call x1, Pallas kernels, on_device(): pl.pallas_call(kernel, out_shape=[out] * 3, in_specs=[vm] * 6, out_specs=...  82.9 us
    unnamed x7, local copies, waits for them, and re-layouts  3.58 us

profile of v2, /device:TPU:1, one launch (start us, length us, event | category | flops | bytes accessed | tf_op | source)
XLA Modules:
  0.0 87.2 jit_solution(18340390625994217552)
XLA Ops:
  0.6 82.9 %vumps.1 = (f32[20,16,256]{2,1,0:T(8,128)}, f32[20,16,256]{2,1,0:T(8,128)}, f32[20,16,256]{2,1,0:T(8,128)}) custom-call(bf16[20,16,256]{2,1,0:T(8,128)(2,1)} %bitcast.31, bf16[20,16,256]{2,1,0:T(8,128)(2,1)} %bitcast.32, bf16[20,16,256]{2,1,0:T(8,128)(2,1)} %bitcast.33, bf16[400,400]{1,0:T(8,128)(2,1)} %bitcast.28, f32[20,16,256]{2,1,0:T(8,128)} %bitcast.29, ...), custom_call_target="tpu_custom_call" | custom-call | flops 8999999488 | bytes 3000000 | tf_op jit(solution)/shard_map/vumps/pallas_call | solution.py:353
  83.6 0.0 copy-start.1
  83.6 1.8 %copy.12 = f32[1,16,20,256]{3,1,2,0:T(8,128)} copy(f32[1,16,20,256]{3,1,2,0:T(8,128)} %bitcast.27) | data formatting | bytes 655360
  85.3 0.0 copy-done.1
  85.3 0.0 copy-start
  85.3 0.7 copy.13
  86.1 0.4 copy-done
  86.4 0.7 copy.14
Async XLA Ops:
  83.6 1.8 %copy-start.1 = (f32[20,16,256]{2,1,0:T(8,128)S(1)}, f32[20,16,256]{2,1,0:T(8,128)}, u32[]{:S(2)}) copy-start(f32[20,16,256]{2,1,0:T(8,128)} %get-tuple-element.7) | copy-start | bytes 983044
  85.3 1.1 %copy-start = (f32[20,16,256]{2,1,0:T(8,128)S(1)}, f32[20,16,256]{2,1,0:T(8,128)}, u32[]{:S(2)}) copy-start(f32[20,16,256]{2,1,0:T(8,128)} %get-tuple-element.8) | copy-start | bytes 983044

commit v3 on v2

--- a/solution.py
+++ b/solution.py
@@ -26,9 +26,9 @@
     new_left_ref, new_right_ref, new_center_ref,
     pad, half_r, p_al, p_ar, lbf, lbp,
     g_al, g_ar, g_ac, g_r, g_n,
-    lb, arj, alt, w2, w4, xs, ys, acc, zf, zk,
+    lb, arj, alt, w2, w4, xs, ys, ys2, acc, zf, zk,
     sib_s, sib_r, x_s, x_r, raw, lp, lr, ln,
-    rs_s, n_in, n_sum, n_snd, n_oth, cy_s, cy_r, sq_s, sq_r, sc_s, sc_r,
+    rs_s, n_in, n_sum, n_snd, n_oth, cy_s, cy_r, sq_s, sq_r,
     send_sem, recv_sem,
 ):
     col = lax.axis_index("col")
@@ -44,7 +44,8 @@
     XP = [at(dx=d) for d in (1, 2, 3)]
 
     barrier = pltpu.get_barrier_semaphore()
-    peers = [SIB, YP] + XP + [at(1), at(1, 1), at(-1), at(-1, 1)]
+    SY = at(dy=1, dc=1)
+    peers = [SIB, YP, SY] + XP + [at(d, 0, k) for d in (1, -1) for k in range(4)] + [at(1, 1), at(-1, 1)]
     for p in peers:
         pl.semaphore_signal(barrier, inc=1, device_id=p, device_id_type=MESH)
 
@@ -97,21 +98,44 @@
             put(1 - y, u, p[u])
         return padded()
 
-    def to_x(ref):
-        return [send(ref, ref, p) for p in XP]
-
     def to_y(g, src):
         return send(src, g.at[c, x, y], YP)
 
+    def both_ways(g, yy):
+        ref = g.at[c, x, yy]
+        return send(ref, ref, XP[0]), send(ref, ref, XP[2])
+
     def own_x(g):
-        return to_x(g.at[c, x, y])
-
-    def rest_x(g, first):
+        return list(both_ways(g, y))
+
+    def rest_x(ring, g, first):
         recv(first)
-        return to_x(g.at[c, x, 1 - y])
-
-    def to_sib(g, xs_):
-        recv(xs_)
+        ring.extend(both_ways(g, 1 - y))
+
+    def hand_up(ring, g):
+        recv(ring[0])
+        ref = g.at[c, (x + 3) % 4, y]
+        ring.append(send(ref, ref, XP[0]))
+
+    def hand_down(ring, g):
+        recv(ring[3])
+        ref = g.at[c, (x + 1) % 4, 1 - y]
+        ring.append(send(ref, ref, XP[2]))
+
+    def to_sib(g, ring):
+        recv([ring[1], ring[2], ring[4], ring[5]])
+        return send(g.at[c], g.at[c], SIB)
+
+    def straight(ref):
+        return [send(ref, ref, p) for p in XP]
+
+    def straight_both(g, first):
+        cps = straight(g.at[c, x, y])
+        recv(first)
+        return cps + straight(g.at[c, x, 1 - y])
+
+    def all_to_sib(g, cps):
+        recv(cps)
         return send(g.at[c], g.at[c], SIB)
 
     g_al[c, x, y] = own_half(al_ref[...])
@@ -128,13 +152,15 @@
     ar_y = to_y(g_ar, lanes(ar_ref, 1 - y))
     p_ar_y = send(lanes(ar_ref, y), p_ar, YP)
     ac_y = to_y(g_ac, lanes(ac_ref, 1 - y))
+    rest_x(al_x, g_al, al_y)
+    hand_up(al_x, g_al)
+    r_x = own_x(g_r)
     g_ar[c, x, y] = own_half(ar_ref[...])
     g_ac[c, x, y] = own_half(ac_ref[...])
-    al_x += rest_x(g_al, al_y)
-    r_x = own_x(g_r) + rest_x(g_r, r_y)
-    ar_x = own_x(g_ar)
     lb[0] = pad_own(l_ref).astype(BF)
     alt[:, :384] = pad_own(al_ref).T.astype(BF)
+    hand_down(al_x, g_al)
+    rest_x(r_x, g_r, r_y)
     arj[0] = pad_own(ar_ref).astype(BF)
     ln[...] = jnp.zeros_like(ln)
 
@@ -158,24 +184,19 @@
     def pair_half(g, u2):
         return jnp.concatenate([full_rows(g, 2 * u2), full_rows(g, 2 * u2 + 1)], axis=1)
 
-    def run(n, body, hooks=()):
-        begin = 0
-        for i, f in list(hooks) + [(n, None)]:
-            lax.fori_loop(begin, i, lambda k, _: body(k), None)
-            begin = i
-            if f is not None:
-                f()
-
-    def step_one(lhs_ref, g, hooks=()):
+    def run(n, body):
+        lax.fori_loop(0, n, lambda k, _: body(k), None)
+
+    def step_one(lhs_ref, g):
         def body(q):
             rhs = jnp.concatenate([pair_half(g, 5 * q + i) for i in range(5)], axis=1)
             for k in range(2):
                 out = dot(lhs_ref[k], rhs)
                 for i in range(5):
                     xs[5 * q + i, 16 * k:16 * k + 16] = out[:, i * CHI:(i + 1) * CHI].reshape(16, DP, CHI)
-        run(D // 2 // 5, body, hooks)
-
-    def step_two(m_ref, hooks=()):
+        run(D // 2 // 5, body)
+
+    def step_two(m_ref, ys, scale=None):
         def body(q):
             cols_ = []
             for i in range(4):
@@ -187,6 +208,8 @@
                     rows.append(jnp.concatenate([v0[:, HALF:], v1[:, HALF:]], axis=1))
                 cols_.append(jnp.concatenate(rows, axis=0).astype(BF))
             both = dot(m_ref[...], jnp.concatenate(cols_, axis=1))
+            if scale is not None:
+                both = both * scale
             for i in range(4):
                 out = both[:, i * CHI:(i + 1) * CHI]
                 for r2 in range(D // 2):
@@ -195,9 +218,9 @@
                     top = jnp.concatenate([o0[:, :HALF], o1[:, :HALF]], axis=1)
                     low = jnp.concatenate([o0[:, HALF:], o1[:, HALF:]], axis=1)
                     ys[r2, 4 * q + i] = jnp.concatenate([top, low], axis=0).astype(BF)
-        run(16 // 4, body, hooks)
-
-    def step_three(g, k):
+        run(16 // 4, body)
+
+    def step_three(g, ys, k):
         def body(n2):
             lhs = jnp.concatenate([ys[i, pl.ds(8 * k, 8)].reshape(384, CHI) for i in range(10)], axis=1)
             rhs = jnp.concatenate([pair_half(g, i) for i in range(10)], axis=1)
@@ -206,20 +229,22 @@
         pad[0] = acc[k, :, :HALF]
         pad[1] = acc[k, :, HALF:]
 
-    def sum_all(part, slot):
+    def sum_a(slot, part):
         sq_s[slot, 0] = part
-        cp = send(sq_s.at[slot, 0], sq_r.at[slot, 0], SIB)
-        recv(cp)
-        part = part + sq_r[slot, 0]
-        sq_s[slot, 1] = part
-        cp = send(sq_s.at[slot, 1], sq_r.at[slot, 1], YP)
-        recv(cp)
-        part = part + sq_r[slot, 1]
-        sq_s[slot, 2] = part
-        cps = [send(sq_s.at[slot, 2], sq_r.at[slot, 2 + d], XP[d]) for d in range(3)]
+        return [send(sq_s.at[slot, 0], sq_r.at[slot, i], p) for i, p in enumerate((SIB, YP, SY))]
+
+    def sum_b(slot, cps, dcol):
         recv(cps)
-        part = part + sq_r[slot, 2] + sq_r[slot, 3] + sq_r[slot, 4]
-        total = jnp.sum(part)
+        sq_s[slot, 1] = sq_s[slot, 0] + sq_r[slot, 0] + sq_r[slot, 1] + sq_r[slot, 2]
+        return [
+            send(sq_s.at[slot, 1], sq_r.at[slot, 3 + d], at(dcol, 0, d))
+            for d in range(4) if d > 0 or dcol != 0
+        ]
+
+    def sum_c(slot, cps):
+        recv(cps)
+        first = sq_r[slot, 3] if len(cps) == 4 else sq_s[slot, 1]
+        total = jnp.sum(first + sq_r[slot, 4] + sq_r[slot, 5] + sq_r[slot, 6])
         return jnp.sqrt(float(CHI * D * CHI) / total)
 
     def squares(v):
@@ -228,30 +253,34 @@
             s = s[:, :HALF] + s[:, HALF:]
         return s[:8] + s[8:]
 
+    recv([p_al_y, lb_y])
+    lb[1] = pad_own(lbp).astype(BF)
+    alt[:, 384:] = pad_partner(g_al, p_al).T.astype(BF)
     al_sib = to_sib(g_al, al_x)
-    ar_x += rest_x(g_ar, ar_y)
-    recv([p_al_y, lb_y])
-    alt[:, 384:] = pad_partner(g_al, p_al).T.astype(BF)
-    lb[1] = pad_own(lbp).astype(BF)
+    hand_up(r_x, g_r)
     recv(al_sib)
+    ar_x = own_x(g_ar)
     step_one(lb, g_al)
-    step_two(w2)
+    hand_down(r_x, g_r)
+    rest_x(ar_x, g_ar, ar_y)
+    step_two(w2, ys)
+    hand_up(ar_x, g_ar)
     r_sib = to_sib(g_r, r_x)
+    sib = []
+    for ch in range(2):
+        rhs = jnp.concatenate([ys[ch * 5 + i].reshape(768, CHI) for i in range(5)], axis=1)
+        out = dot(alt[...], rhs)
+        for i in range(5):
+            r2 = ch * 5 + i
+            zf[...] = out[:, i * CHI:(i + 1) * CHI].reshape(8, 2, ROWS, CHI)
+            sib_s[r2] = zf[:, 1 - c].astype(BF)
+            zk[r2] = zf[:, c]
+        part_of = pl.ds(ch * 5, 5)
+        sib.append(send(sib_s.at[part_of], sib_r.at[part_of], SIB))
+
     recv(p_ar_y)
     arj[1] = pad_partner(g_ar, p_ar).astype(BF)
-    sib = []
-    for ch in range(2):
-        def z_body(k):
-            rhs = jnp.concatenate([ys[ch * 5 + 5 * k + i].reshape(768, CHI) for i in range(5)], axis=1)
-            out = dot(alt[...], rhs)
-            for i in range(5):
-                r2 = ch * 5 + 5 * k + i
-                zf[...] = out[:, i * CHI:(i + 1) * CHI].reshape(8, 2, ROWS, CHI)
-                sib_s[r2] = zf[:, 1 - c].astype(BF)
-                zk[r2] = zf[:, c]
-        run(5 // 5, z_body)
-        part_of = pl.ds(ch * 5, 5)
-        sib.append(send(sib_s.at[part_of], sib_r.at[part_of], SIB))
+    hand_down(ar_x, g_ar)
     rs = []
     for ch in range(2):
         recv(sib[ch])
@@ -266,11 +295,25 @@
         for d in (1, 2, 3):
             to = (x + d) % 4
             rs.append(send(x_s.at[to, part_of], x_r.at[d - 1, part_of], XP[d - 1]))
-    ac_x = own_x(g_ac) + rest_x(g_ac, ac_y)
-
     recv(r_sib)
     step_one(arj, g_r)
-    step_two(w4, [(2, lambda: None)])
+    step_two(w4, ys2)
+    ar_sib = to_sib(g_ar, ar_x)
+    ac_x = straight_both(g_ac, ac_y)
+
+    def right_block(yy):
+        k = (y + yy) % 2
+        step_three(g_ar, ys2, k)
+        for h in range(2):
+            for l in range(D):
+                rs_s[h, yy, l] = row(h, l).astype(BF)
+        return [
+            send(rs_s.at[y, yy], n_in.at[y, yy], at(-1)),
+            send(rs_s.at[1 - y, yy], n_in.at[y, yy], at(-1, 1)),
+        ]
+
+    recv(ar_sib)
+    n_col = [right_block(0), right_block(1)]
     recv(rs)
     part = jnp.zeros((8, HALF), F32)
     for r2 in range(D // 2):
@@ -281,61 +324,52 @@
             lp[r2, yy] = v.astype(BF)
             part = part + squares(v)
     l_col = [send(lp, lr.at[y], at(1)), send(lp, lr.at[y], at(1, 1))]
-    left_part = part
-    ar_sib = to_sib(g_ar, ar_x)
-    scale = sum_all(left_part, 1)
-    sc_s[...] = jnp.full((8, HALF), 1.0, F32) * scale
-    l_sc = send(sc_s, sc_r, at(1))
-    recv(ar_sib)
-    n_col = []
-    for k, blk in ((0, y), (1, 1 - y)):
-        step_three(g_ar, k)
-        for h in range(2):
-            for l in range(D):
-                rs_s[h, k, l] = row(h, l).astype(BF)
-        n_col.append(send(rs_s.at[y, k], n_in.at[y, blk], at(-1)))
-        n_col.append(send(rs_s.at[1 - y, k], n_in.at[y, blk], at(-1, 1)))
-
-    ac_sib = to_sib(g_ac, ac_x)
-    recv(l_col + [l_sc])
-    scale = sc_r[0:1, 0:1]
-    for l in range(D):
-        h = l % 2
-        for src in range(2):
-            for yy in range(2):
-                v = lr[src, l // 2, yy, :, h * HALF:(h + 1) * HALF].astype(F32) * scale
-                ln[yy, src, pl.ds(l, ROWS, stride=DP), :] = v
+    left_sum = sum_b(1, sum_a(1, part), 1)
+
+    part = jnp.zeros((8, HALF), F32)
+    n_x = []
     for yy in range(2):
-        lb[yy] = jnp.concatenate([ln[yy, 0], ln[yy, 1]], axis=1).astype(BF)
-    for l in range(D):
-        for src in range(2):
-            new_left_ref[l, :, src * HALF:(src + 1) * HALF] = ln[y, src, pl.ds(l, ROWS, stride=DP), :]
-    recv(ac_sib)
-    step_one(lb, g_ac)
-    recv(n_col)
-    part = jnp.zeros((8, HALF), F32)
-    for yy in range(2):
+        recv(n_col[yy])
         for l in range(D):
             v = n_in[0, yy, l].astype(F32) + n_in[1, yy, l].astype(F32)
             n_sum[yy, l] = v
             g_n[c, x, yy, l] = v.astype(BF)
             part = part + squares(v)
-    n_x = to_x(g_n.at[c, x])
+        n_x += straight(g_n.at[c, x, yy])
     n_snd[...] = n_sum[1 - y].astype(BF)
     n_y = send(n_snd, n_oth, YP)
-    step_two(w2)
-    n_sib = to_sib(g_n, n_x)
-    scale = sum_all(part, 0)
+    right_sum = sum_a(0, part)
+    ac_sib = all_to_sib(g_ac, ac_x)
+    recv(l_col)
+    for l in range(D):
+        h = l % 2
+        for src in range(2):
+            for yy in range(2):
+                v = lr[src, l // 2, yy, :, h * HALF:(h + 1) * HALF].astype(F32)
+                ln[yy, src, pl.ds(l, ROWS, stride=DP), :] = v
+    for yy in range(2):
+        lb[yy] = jnp.concatenate([ln[yy, 0], ln[yy, 1]], axis=1).astype(BF)
+    right_sum = sum_b(0, right_sum, 0)
+    recv(ac_sib)
+    step_one(lb, g_ac)
+    scale = sum_c(1, left_sum)
+    step_two(w2, ys, scale)
+    n_sib = all_to_sib(g_n, n_x)
+    for l in range(D):
+        for src in range(2):
+            v = ln[y, src, pl.ds(l, ROWS, stride=DP), :] * scale
+            new_left_ref[l, :, src * HALF:(src + 1) * HALF] = v
+    recv(n_sib)
+    step_three(g_n, ys, 1 - y)
+    cy_s[...] = acc[1 - y].astype(BF)
+    cy = send(cy_s, cy_r, YP)
+    step_three(g_n, ys, y)
+    scale = sum_c(0, right_sum)
     recv(n_y)
     for l in range(D):
         a, b = n_sum[y, l] * scale, n_oth[l].astype(F32) * scale
         new_right_ref[l, :, :HALF] = jnp.where(y == 0, a, b)
         new_right_ref[l, :, HALF:] = jnp.where(y == 0, b, a)
-    recv(n_sib)
-    step_three(g_n, 1 - y)
-    cy_s[...] = acc[1 - y].astype(BF)
-    cy = send(cy_s, cy_r, YP)
-    step_three(g_n, y)
     recv(cy)
     pad[0] = (acc[y, :, :HALF] + cy_r[:, :HALF].astype(F32)) * scale
     pad[1] = (acc[y, :, HALF:] + cy_r[:, HALF:].astype(F32)) * scale
@@ -364,7 +398,7 @@
             V((CHI, 2 * ROWS * DP), BF),
             V((D * DP, D * DP), BF), V((D * DP, D * DP), BF),
             V((D // 2, 32, DP, CHI), F32),
-            V((D // 2, 16, 2 * DP, CHI), BF),
+            *[V((D // 2, 16, 2 * DP, CHI), BF)] * 2,
             V((2, ROWS * DP, CHI), F32),
             V((8, 2, ROWS, CHI), F32),
             V((D // 2, 8, ROWS, CHI), F32),
@@ -377,9 +411,8 @@
             V((2, D, ROWS, HALF), F32),
             V((D, ROWS, HALF), BF), V((D, ROWS, HALF), BF),
             V((ROWS * DP, CHI), BF), V((ROWS * DP, CHI), BF),
-            V((2, 3, 8, HALF), F32), V((2, 5, 8, HALF), F32),
-            V((8, HALF), F32), V((8, HALF), F32),
-            pltpu.SemaphoreType.DMA((72,)), pltpu.SemaphoreType.DMA((72,)),
+            V((2, 2, 8, HALF), F32), V((2, 7, 8, HALF), F32),
+            pltpu.SemaphoreType.DMA((80,)), pltpu.SemaphoreType.DMA((80,)),
         ],
         compiler_params=pltpu.CompilerParams(
             collective_id=0, has_side_effects=True, vmem_limit_bytes=56 * 2**20

time: 88.6 us -> 78.9 us (0.89); the launches traced: 87.2 us -> 78.7 us
  Pallas kernels: 82.9 us -> 74.5 us
    pallas_call x1, Pallas kernels: 82.9 us -> 74.5 us  [on_device(): pl.pallas_call(kernel, out_shape=[out] * 3, in_specs=[vm] * 6, out_specs=...]
where the time goes in v3:
time: 78.9 us; the launch traced here: 78.7 us
  Pallas kernels  74.5 us (94%)
  local copies, waits for them, and re-layouts  3.58 us (5%)
    pallas_call x1, Pallas kernels, on_device(): pl.pallas_call(kernel, out_shape=[out] * 3, in_specs=[vm] * 6, out_specs=...  74.5 us
    unnamed x7, local copies, waits for them, and re-layouts  3.58 us

profile of v3, /device:TPU:1, one launch (start us, length us, event | category | flops | bytes accessed | tf_op | source)
XLA Modules:
  0.0 78.7 jit_solution(8292853742829266552)
XLA Ops:
  0.6 74.5 %vumps.1 = (f32[20,16,256]{2,1,0:T(8,128)}, f32[20,16,256]{2,1,0:T(8,128)}, f32[20,16,256]{2,1,0:T(8,128)}) custom-call(bf16[20,16,256]{2,1,0:T(8,128)(2,1)} %bitcast.31, bf16[20,16,256]{2,1,0:T(8,128)(2,1)} %bitcast.32, bf16[20,16,256]{2,1,0:T(8,128)(2,1)} %bitcast.33, bf16[400,400]{1,0:T(8,128)(2,1)} %bitcast.28, f32[20,16,256]{2,1,0:T(8,128)} %bitcast.29, ...), custom_call_target="tpu_custom_call" | custom-call | flops 8999999488 | bytes 3000000 | tf_op jit(solution)/shard_map/vumps/pallas_call | solution.py:387
  75.1 0.0 copy-start.1
  75.1 1.8 %copy.12 = f32[1,16,20,256]{3,1,2,0:T(8,128)} copy(f32[1,16,20,256]{3,1,2,0:T(8,128)} %bitcast.27) | data formatting | bytes 655360
  76.9 0.0 copy-done.1
  76.9 0.0 copy-start
  76.9 0.7 copy.13
  77.6 0.4 copy-done
  78.0 0.7 copy.14
Async XLA Ops:
  75.1 1.8 %copy-start.1 = (f32[20,16,256]{2,1,0:T(8,128)S(1)}, f32[20,16,256]{2,1,0:T(8,128)}, u32[]{:S(2)}) copy-start(f32[20,16,256]{2,1,0:T(8,128)} %get-tuple-element.7) | copy-start | bytes 983044
  76.9 1.1 %copy-start = (f32[20,16,256]{2,1,0:T(8,128)S(1)}, f32[20,16,256]{2,1,0:T(8,128)}, u32[]{:S(2)}) copy-start(f32[20,16,256]{2,1,0:T(8,128)} %get-tuple-element.8) | copy-start | bytes 983044

commit v4 on v3

--- a/solution.py
+++ b/solution.py
@@ -28,7 +28,7 @@
     g_al, g_ar, g_ac, g_r, g_n,
     lb, arj, alt, w2, w4, xs, ys, ys2, acc, zf, zk,
     sib_s, sib_r, x_s, x_r, raw, lp, lr, ln,
-    rs_s, n_in, n_sum, n_snd, n_oth, cy_s, cy_r, sq_s, sq_r,
+    rs_s, n_in, n_sum, n_snd, n_oth, cy_s, cy_r, sq_s, sq_r, sc_s, sc_r,
     send_sem, recv_sem,
 ):
     col = lax.axis_index("col")
@@ -45,7 +45,7 @@
 
     barrier = pltpu.get_barrier_semaphore()
     SY = at(dy=1, dc=1)
-    peers = [SIB, YP, SY] + XP + [at(d, 0, k) for d in (1, -1) for k in range(4)] + [at(1, 1), at(-1, 1)]
+    peers = [SIB, YP, SY] + XP + [at(1), at(1, 1), at(-1), at(-1, 1)]
     for p in peers:
         pl.semaphore_signal(barrier, inc=1, device_id=p, device_id_type=MESH)
 
@@ -233,18 +233,14 @@
         sq_s[slot, 0] = part
         return [send(sq_s.at[slot, 0], sq_r.at[slot, i], p) for i, p in enumerate((SIB, YP, SY))]
 
-    def sum_b(slot, cps, dcol):
+    def sum_b(slot, cps):
         recv(cps)
         sq_s[slot, 1] = sq_s[slot, 0] + sq_r[slot, 0] + sq_r[slot, 1] + sq_r[slot, 2]
-        return [
-            send(sq_s.at[slot, 1], sq_r.at[slot, 3 + d], at(dcol, 0, d))
-            for d in range(4) if d > 0 or dcol != 0
-        ]
+        return [send(sq_s.at[slot, 1], sq_r.at[slot, 3 + d], XP[d]) for d in range(3)]
 
     def sum_c(slot, cps):
         recv(cps)
-        first = sq_r[slot, 3] if len(cps) == 4 else sq_s[slot, 1]
-        total = jnp.sum(first + sq_r[slot, 4] + sq_r[slot, 5] + sq_r[slot, 6])
+        total = jnp.sum(sq_s[slot, 1] + sq_r[slot, 3] + sq_r[slot, 4] + sq_r[slot, 5])
         return jnp.sqrt(float(CHI * D * CHI) / total)
 
     def squares(v):
@@ -297,9 +293,9 @@
             rs.append(send(x_s.at[to, part_of], x_r.at[d - 1, part_of], XP[d - 1]))
     recv(r_sib)
     step_one(arj, g_r)
-    step_two(w4, ys2)
     ar_sib = to_sib(g_ar, ar_x)
     ac_x = straight_both(g_ac, ac_y)
+    step_two(w4, ys2)
 
     def right_block(yy):
         k = (y + yy) % 2
@@ -324,7 +320,7 @@
             lp[r2, yy] = v.astype(BF)
             part = part + squares(v)
     l_col = [send(lp, lr.at[y], at(1)), send(lp, lr.at[y], at(1, 1))]
-    left_sum = sum_b(1, sum_a(1, part), 1)
+    left_sum = sum_b(1, sum_a(1, part))
 
     part = jnp.zeros((8, HALF), F32)
     n_x = []
@@ -339,6 +335,8 @@
     n_snd[...] = n_sum[1 - y].astype(BF)
     n_y = send(n_snd, n_oth, YP)
     right_sum = sum_a(0, part)
+    sc_s[...] = jnp.full((8, HALF), 1.0, F32) * sum_c(1, left_sum)
+    l_sc = send(sc_s, sc_r, at(1))
     ac_sib = all_to_sib(g_ac, ac_x)
     recv(l_col)
     for l in range(D):
@@ -349,39 +347,43 @@
                 ln[yy, src, pl.ds(l, ROWS, stride=DP), :] = v
     for yy in range(2):
         lb[yy] = jnp.concatenate([ln[yy, 0], ln[yy, 1]], axis=1).astype(BF)
-    right_sum = sum_b(0, right_sum, 0)
+    right_sum = sum_b(0, right_sum)
     recv(ac_sib)
     step_one(lb, g_ac)
-    scale = sum_c(1, left_sum)
+    recv(l_sc)
+    scale = sc_r[0:1, 0:1]
     step_two(w2, ys, scale)
-    n_sib = all_to_sib(g_n, n_x)
+    n_sib = []
+    for yy in range(2):
+        recv(n_x[3 * yy:3 * yy + 3])
+        ref = g_n.at[c, :, yy]
+        n_sib.append(send(ref, ref, SIB))
     for l in range(D):
         for src in range(2):
             v = ln[y, src, pl.ds(l, ROWS, stride=DP), :] * scale
-            new_left_ref[l, :, src * HALF:(src + 1) * HALF] = v
+            new_left_ref[l, :, src * HALF:(src + 1) * HALF] = v.astype(BF)
     recv(n_sib)
     step_three(g_n, ys, 1 - y)
-    cy_s[...] = acc[1 - y].astype(BF)
+    for n in range(D):
+        cy_s[n] = jnp.concatenate([row(0, n), row(1, n)], axis=1).astype(BF)
     cy = send(cy_s, cy_r, YP)
     step_three(g_n, ys, y)
     scale = sum_c(0, right_sum)
     recv(n_y)
     for l in range(D):
         a, b = n_sum[y, l] * scale, n_oth[l].astype(F32) * scale
-        new_right_ref[l, :, :HALF] = jnp.where(y == 0, a, b)
-        new_right_ref[l, :, HALF:] = jnp.where(y == 0, b, a)
+        new_right_ref[l, :, :HALF] = jnp.where(y == 0, a, b).astype(BF)
+        new_right_ref[l, :, HALF:] = jnp.where(y == 0, b, a).astype(BF)
     recv(cy)
-    pad[0] = (acc[y, :, :HALF] + cy_r[:, :HALF].astype(F32)) * scale
-    pad[1] = (acc[y, :, HALF:] + cy_r[:, HALF:].astype(F32)) * scale
     for n in range(D):
-        new_center_ref[n, :, :HALF] = row(0, n)
-        new_center_ref[n, :, HALF:] = row(1, n)
+        v = jnp.concatenate([row(0, n), row(1, n)], axis=1) + cy_r[n].astype(F32)
+        new_center_ref[n] = (v * scale).astype(BF)
     for cp in started:
         cp.wait_send()
 
 
 def on_device(left_iso, right_iso, center, site_tensor, left_env, right_env):
-    out = jax.ShapeDtypeStruct((D, ROWS, CHI), F32)
+    out = jax.ShapeDtypeStruct((D, ROWS, CHI), BF)
     vm = pl.BlockSpec(memory_space=pltpu.VMEM)
     V = pltpu.VMEM
     res = pl.pallas_call(
@@ -410,8 +412,9 @@
             V((2, 2, D, ROWS, HALF), BF), V((2, 2, D, ROWS, HALF), BF),
             V((2, D, ROWS, HALF), F32),
             V((D, ROWS, HALF), BF), V((D, ROWS, HALF), BF),
-            V((ROWS * DP, CHI), BF), V((ROWS * DP, CHI), BF),
-            V((2, 2, 8, HALF), F32), V((2, 7, 8, HALF), F32),
+            V((D, ROWS, CHI), BF), V((D, ROWS, CHI), BF),
+            V((2, 2, 8, HALF), F32), V((2, 6, 8, HALF), F32),
+            V((8, HALF), F32), V((8, HALF), F32),
             pltpu.SemaphoreType.DMA((80,)), pltpu.SemaphoreType.DMA((80,)),
         ],
         compiler_params=pltpu.CompilerParams(
@@ -424,7 +427,7 @@
         site_tensor[0],
         *(v[0].transpose(1, 0, 2) for v in (left_env, right_env)),
     )
-    return tuple(o.transpose(1, 0, 2)[None] for o in res)
+    return tuple(o.astype(F32).transpose(1, 0, 2)[None] for o in res)
 
 
 def solution(mesh):

time: 78.9 us -> 75.7 us (0.959)
  local copies, waits for them, and re-layouts: 3.58 us -> 0.01 us
  other arithmetic: 0 us -> 2.7 us
  Pallas kernels: 74.5 us -> 72.2 us
    unnamed x7 -> x2, local copies, waits for them, and re-layouts: 3.58 us -> 0.01 us
    broadcast_in_dim x0 -> x2, other arithmetic: none -> 2.7 us  [on_device(): return tuple((o.astype(F32).transpose(1, 0, 2)[None] for o in res))]
    pallas_call x1, Pallas kernels: 74.5 us -> 72.2 us  [on_device(): pl.pallas_call(kernel, out_shape=[out] * 3, in_specs=[vm] * 6, out_specs=...]
where the time goes in v4:
time: 75.7 us; the launch traced here: 75.6 us
  Pallas kernels  72.2 us (95%)
  other arithmetic  2.7 us (4%)
    pallas_call x1, Pallas kernels, on_device(): pl.pallas_call(kernel, out_shape=[out] * 3, in_specs=[vm] * 6, out_specs=...  72.2 us
    broadcast_in_dim x2, other arithmetic, on_device(): return tuple((o.astype(F32).transpose(1, 0, 2)[None] for o in res))  2.7 us

profile of v4, /device:TPU:1, one launch (start us, length us, event | category | flops | bytes accessed | tf_op | source)
XLA Modules:
  0.0 75.6 jit_solution(17750210783420844955)
XLA Ops:
  0.6 72.2 %vumps.1 = (bf16[20,16,256]{2,1,0:T(8,128)(2,1)}, bf16[20,16,256]{2,1,0:T(8,128)(2,1)}, bf16[20,16,256]{2,1,0:T(8,128)(2,1)}) custom-call(bf16[20,16,256]{2,1,0:T(8,128)(2,1)} %bitcast.31, bf16[20,16,256]{2,1,0:T(8,128)(2,1)} %bitcast.32, bf16[20,16,256]{2,1,0:T(8,128)(2,1)} %bitcast.33, bf16[400,400]{1,0:T(8,128)(2,1)} %bitcast.28, ...), custom_call_target="tpu_custom_call" | custom-call | flops 8999999488 | bytes 3000000 | tf_op jit(solution)/shard_map/vumps/pallas_call | solution.py:389
  72.9 0.0 copy-start
  72.9 1.9 %convert_bitcast_fusion = (f32[1,16,20,256]{3,1,2,0:T(8,128)}, f32[1,16,20,256]{3,1,2,0:T(8,128)}) fusion(bf16[20,16,256]{2,1,0:T(8,128)(2,1)} %get-tuple-element.8, bf16[20,16,256]{2,1,0:T(8,128)(2,1)} %get-tuple-element.7), kind=kLoop, calls=%fused_computation | loop fusion | flops 163840 | bytes 983040 | tf_op jit(solution)/shard_map/broadcast_in_dim | solution.py:430
  74.8 0.0 copy-done
  74.8 0.8 %convert_bitcast_fusion.2 = f32[1,16,20,256]{3,1,2,0:T(8,128)} fusion(bf16[20,16,256]{2,1,0:T(8,128)(2,1)S(1)} %copy-done), kind=kLoop, calls=%fused_computation.2 | loop fusion | flops 81920 | bytes 491520 | tf_op jit(solution)/shard_map/broadcast_in_dim | solution.py:430
Async XLA Ops:
  72.9 2.0 %copy-start = (bf16[20,16,256]{2,1,0:T(8,128)(2,1)S(1)}, bf16[20,16,256]{2,1,0:T(8,128)(2,1)}, u32[]{:S(2)}) copy-start(bf16[20,16,256]{2,1,0:T(8,128)(2,1)} %get-tuple-element.6) | copy-start | bytes 491524

commit v5 on v4

--- a/solution.py
+++ b/solution.py
@@ -199,8 +199,8 @@
     def step_two(m_ref, ys, scale=None):
         def body(q):
             cols_ = []
-            for i in range(4):
-                p = 4 * q + i
+            for i in range(8):
+                p = 8 * q + i
                 rows = []
                 for u2 in range(D // 2):
                     v0, v1 = xs[u2, 2 * p], xs[u2, 2 * p + 1]
@@ -210,15 +210,15 @@
             both = dot(m_ref[...], jnp.concatenate(cols_, axis=1))
             if scale is not None:
                 both = both * scale
-            for i in range(4):
+            for i in range(8):
                 out = both[:, i * CHI:(i + 1) * CHI]
                 for r2 in range(D // 2):
                     o0 = out[2 * r2 * DP:(2 * r2 + 1) * DP]
                     o1 = out[(2 * r2 + 1) * DP:(2 * r2 + 2) * DP]
                     top = jnp.concatenate([o0[:, :HALF], o1[:, :HALF]], axis=1)
                     low = jnp.concatenate([o0[:, HALF:], o1[:, HALF:]], axis=1)
-                    ys[r2, 4 * q + i] = jnp.concatenate([top, low], axis=0).astype(BF)
-        run(16 // 4, body)
+                    ys[r2, 8 * q + i] = jnp.concatenate([top, low], axis=0).astype(BF)
+        run(16 // 8, body)
 
     def step_three(g, ys, k):
         def body(n2):

time: 75.7 us -> 76 us (level)
  no operation moved by 1% of the time
where the time goes in v5:
time: 76 us; the launch traced here: 75.9 us
  Pallas kernels  72.5 us (95%)
  other arithmetic  2.7 us (4%)
    pallas_call x1, Pallas kernels, on_device(): pl.pallas_call(kernel, out_shape=[out] * 3, in_specs=[vm] * 6, out_specs=...  72.5 us
    broadcast_in_dim x2, other arithmetic, on_device(): return tuple((o.astype(F32).transpose(1, 0, 2)[None] for o in res))  2.7 us

profile of v5, /device:TPU:1, one launch (start us, length us, event | category | flops | bytes accessed | tf_op | source)
XLA Modules:
  0.0 75.9 jit_solution(3087253142451051771)
XLA Ops:
  0.6 72.5 %vumps.1 = (bf16[20,16,256]{2,1,0:T(8,128)(2,1)}, bf16[20,16,256]{2,1,0:T(8,128)(2,1)}, bf16[20,16,256]{2,1,0:T(8,128)(2,1)}) custom-call(bf16[20,16,256]{2,1,0:T(8,128)(2,1)} %bitcast.31, bf16[20,16,256]{2,1,0:T(8,128)(2,1)} %bitcast.32, bf16[20,16,256]{2,1,0:T(8,128)(2,1)} %bitcast.33, bf16[400,400]{1,0:T(8,128)(2,1)} %bitcast.28, ...), custom_call_target="tpu_custom_call" | custom-call | flops 8999999488 | bytes 3000000 | tf_op jit(solution)/shard_map/vumps/pallas_call | solution.py:389
  73.2 0.0 copy-start
  73.2 1.9 %convert_bitcast_fusion = (f32[1,16,20,256]{3,1,2,0:T(8,128)}, f32[1,16,20,256]{3,1,2,0:T(8,128)}) fusion(bf16[20,16,256]{2,1,0:T(8,128)(2,1)} %get-tuple-element.8, bf16[20,16,256]{2,1,0:T(8,128)(2,1)} %get-tuple-element.7), kind=kLoop, calls=%fused_computation | loop fusion | flops 163840 | bytes 983040 | tf_op jit(solution)/shard_map/broadcast_in_dim | solution.py:430
  75.1 0.0 copy-done
  75.1 0.8 convert_bitcast_fusion.2
Async XLA Ops:
  73.2 2.0 %copy-start = (bf16[20,16,256]{2,1,0:T(8,128)(2,1)S(1)}, bf16[20,16,256]{2,1,0:T(8,128)(2,1)}, u32[]{:S(2)}) copy-start(bf16[20,16,256]{2,1,0:T(8,128)(2,1)} %get-tuple-element.6) | copy-start | bytes 491524
